TPU v7x, 128 devices: a whole 4x4x4 slice. The times are simulated.
128 devices in a mesh: dp: 8 (over z, core), expert: 16 (over y, x).
Axes of the slice: x: 4, y: 4, z: 4, core: 2. Of those that a mesh axis runs over, the one named last changes fastest.
Arguments:
- tokens: bfloat16 [32768, 1024], P(('dp', 'expert')), may hold values from -6 to 6
- cotangent: bfloat16 [32768, 1024], P(('dp', 'expert')), may hold values from -6 to 6
- combine: float32 [32768, 2], P(('dp', 'expert')), may hold values from 0.2 to 1
- expert_ids: int32 [32768, 2], P(('dp', 'expert')), may hold values from 0 to 31, all different within a row; in each aligned block of 256 rows (0 to 255, 256 to 511, ...) at most 32 rows name the same one
- capacity: int32 [32], replicated, may hold values from 16 to 32, as said below
- weight_in: bfloat16 [1024, 32, 2048], P(None, 'expert'), may hold values from -0.1875 to 0.1875
- weight_down: bfloat16 [1024, 32, 1024], P(None, 'expert'), may hold values from -0.1875 to 0.1875
Outputs:
- token_grad: bfloat16 [32768, 1024], P(('dp', 'expert'))
- combine_grad: bfloat16 [32768, 2], P(('dp', 'expert'))
- inner_grad: float32 [1024, 32, 2048], P('dp', 'expert')
- down_grad: float32 [1024, 32, 1024], P('dp', 'expert')
Inputs may be any that keep to these rules, and one draw needn't show every extreme that they name: Some expert has capacity 32. `expert_ids`: in the 256 rows of one device no expert is named more than 32 times.
All inputs are finite; a program needn't handle non-finite values.
Results may differ from a plain program's by a relative error of at most 0.015.
Values may be sent and summed in bfloat16 or wider, within the bound.
A program may use at most 128 MiB of HBM per device.

v0:
```python
import jax
import jax.numpy as jnp
from jax import lax
from jax.sharding import PartitionSpec as P

CAP = 32


def weight_sums(slot_x, dpre, hidden, scaled):
    inner = lax.psum_scatter(
        jnp.einsum("secd,secf->def", slot_x, dpre, preferred_element_type=jnp.float32).astype(
            jnp.bfloat16
        ),
        "dp",
        scatter_dimension=0,
        tiled=True,
    ).astype(jnp.float32)
    down = lax.psum_scatter(
        jnp.einsum("secf,secd->fed", hidden, scaled, preferred_element_type=jnp.float32).astype(
            jnp.bfloat16
        ),
        "dp",
        scatter_dimension=0,
        tiled=True,
    ).astype(jnp.float32)
    return (inner, down)


def on_device(tokens, cotangent, combine, expert_ids, capacity, weight_in, weight_down):
    tok_rows, model_width = tokens.shape
    hidden_width = weight_down.shape[0]
    exp_local = weight_in.shape[1]
    peers = lax.axis_size("expert")
    experts = exp_local * peers
    slots = CAP
    flat_ids = expert_ids.reshape(-1)
    onehot = (flat_ids[:, None] == jnp.arange(experts, dtype=jnp.int32)[None, :]).astype(jnp.int32)
    before = jnp.cumsum(onehot, axis=0) - onehot
    position = jnp.sum(before * onehot, axis=1)
    limit = jnp.sum(onehot * capacity[None, :], axis=1)
    target = jnp.where(position < limit, flat_ids * slots + position, experts * slots)
    assigns = 2 * tok_rows
    source = jnp.full((experts * slots + 1,), assigns, jnp.int32)
    source = source.at[target].set(jnp.arange(assigns, dtype=jnp.int32))[: experts * slots]
    token_of = source // 2
    zero_row = jnp.zeros((1, model_width), jnp.bfloat16)
    send_x = jnp.concatenate([tokens, zero_row], axis=0)[token_of]
    send_dy = jnp.concatenate([cotangent, zero_row], axis=0)[token_of]
    send_c = jnp.concatenate([combine.reshape(-1), jnp.zeros((1,), jnp.float32)], axis=0)[
        source
    ].astype(jnp.bfloat16)
    send_x = send_x.reshape(peers, exp_local * slots, model_width)
    send_dy = send_dy.reshape(peers, exp_local * slots, model_width)
    send_c = send_c.reshape(peers, exp_local * slots)
    recv_x, recv_dy, recv_c = (
        lax.all_to_all(send_x, "expert", split_axis=0, concat_axis=0, tiled=True),
        lax.all_to_all(send_dy, "expert", split_axis=0, concat_axis=0, tiled=True),
        lax.all_to_all(send_c, "expert", split_axis=0, concat_axis=0, tiled=True),
    )
    slot_x = recv_x.reshape(peers, exp_local, slots, model_width)
    slot_dy = recv_dy.reshape(peers, exp_local, slots, model_width)
    slot_c = recv_c.reshape(peers, exp_local, slots)
    pre = jnp.einsum("secd,def->secf", slot_x, weight_in, preferred_element_type=jnp.float32)
    gate = pre[..., :hidden_width]
    upper = pre[..., hidden_width:]
    sig = jax.nn.sigmoid(gate)
    act = gate * sig
    hidden = (act * upper).astype(jnp.bfloat16)
    output = jnp.einsum("secf,fed->secd", hidden, weight_down, preferred_element_type=jnp.float32)
    comb_slot = jnp.sum(slot_dy.astype(jnp.float32) * output, axis=-1).astype(jnp.bfloat16)
    scaled = (slot_c.astype(jnp.float32)[..., None] * slot_dy.astype(jnp.float32)).astype(
        jnp.bfloat16
    )
    dhidden = jnp.einsum("secd,fed->secf", scaled, weight_down, preferred_element_type=jnp.float32)
    dgate = dhidden * upper * sig * (1.0 + gate * (1.0 - sig))
    dpre = jnp.concatenate([dgate, dhidden * act], axis=-1).astype(jnp.bfloat16)
    slot_grad = jnp.einsum(
        "secf,def->secd", dpre, weight_in, preferred_element_type=jnp.float32
    ).astype(jnp.bfloat16)
    back_x, back_c = (
        lax.all_to_all(
            slot_grad.reshape(peers, exp_local * slots, model_width),
            "expert",
            split_axis=0,
            concat_axis=0,
            tiled=True,
        ),
        lax.all_to_all(
            comb_slot.reshape(peers, exp_local * slots),
            "expert",
            split_axis=0,
            concat_axis=0,
            tiled=True,
        ),
    )
    flat_back = jnp.concatenate([back_x.reshape(experts * slots, model_width), zero_row], axis=0)
    flat_comb = jnp.concatenate(
        [back_c.reshape(experts * slots), jnp.zeros((1,), jnp.bfloat16)], axis=0
    )
    per_assign = flat_back[target].astype(jnp.float32).reshape(tok_rows, 2, model_width)
    token_grad = jnp.sum(per_assign, axis=1).astype(jnp.bfloat16)
    combine_grad = flat_comb[target].reshape(tok_rows, 2)
    inner, down = weight_sums(slot_x, dpre, hidden, scaled)
    return (token_grad, combine_grad, inner, down)


def solution(mesh):
    placed = (
        P(("dp", "expert"), None),
        P(("dp", "expert"), None),
        P(("dp", "expert"), None),
        P(("dp", "expert"), None),
        P(),
        P(None, "expert", None),
        P(None, "expert", None),
    )
    return jax.shard_map(
        on_device,
        mesh=mesh,
        in_specs=placed,
        out_specs=(
            P(("dp", "expert"), None),
            P(("dp", "expert"), None),
            P("dp", "expert", None),
            P("dp", "expert", None),
        ),
        check_vma=False,
    )
```

profile of v0, /device:TPU:1, one launch (start us, length us, event | category | flops | bytes accessed | tf_op | source)
XLA Modules:
  0.0 232.5 jit_solution(4830334599722900365)
XLA Ops:
  7.2 0.7 broadcast_multiply_fusion
  7.9 0.8 copy.55
  8.7 0.1 eq.29
  8.8 0.1 eq.25
  9.0 0.8 copy.54
  9.8 0.1 reshape.134
  9.9 0.1 copy.58
  10.1 0.1 mul.64
  10.2 1.2 reduce-window.6
  11.4 0.2 slice_reduce_fusion
  11.7 0.8 select_reduce_fusion
  12.5 2.5 %scatter_custom_fusion = s32[1025]{0:T(1024)S(1)} fusion(s32[512]{0:T(512)S(1)} %bitcast.85, s32[512]{0:T(512)S(1)} %iota.11, s32[]{:T(128)} %constant.15.clone.1), kind=kCustom, calls=%fused_computation.62 | custom fusion | bytes 4104 | tf_op jit(solution)/shard_map/scatter | solution.py:44
  15.0 6.8 %gather_fusion = bf16[1024]{0:T(1024)(128)(2,1)S(1)} fusion(bf16[513]{0:T(1024)(128)(2,1)S(1)} %pad_maximum_fusion.5, s32[1024]{0:T(1024)S(1)} %get-tuple-element.26), kind=kCustom, calls=%fused_computation | custom fusion | bytes 8192 | tf_op jit(solution)/shard_map/gather | solution.py:49
  21.8 0.7 convert_element_type.108
  22.4 7.6 %all-to-all-start = ((bf16[16,1,64]{2,1,0:T(2,128)(2,1)}), bf16[16,1,64]{2,1,0:T(2,128)(2,1)S(1)}, u32[]{:S(2)}, u32[]{:S(2)}) async-start(bf16[16,1,64]{2,1,0:T(2,128)(2,1)} %convert_element_type.108), calls=%async_computation | async-start | bytes 16384 | tf_op jit(solution)/shard_map/all_to_all | solution.py:58
  30.0 1.1 concatenate.21
  31.1 5.3 %gather_fusion.2 = bf16[1024,1024]{1,0:T(8,128)(2,1)} fusion(bf16[257,1024]{1,0:T(8,128)(2,1)S(1)} %concatenate.21, s32[1024]{0:T(1024)S(1)} %get-tuple-element.25), kind=kCustom, calls=%fused_computation.2 | custom fusion | bytes 4198400 | tf_op jit(solution)/shard_map/gather | solution.py:47
  36.5 0.0 copy-start.1
  36.5 0.0 all-to-all-done
  36.5 6.8 %all-to-all-start.2 = ((bf16[16,64,1024]{2,1,0:T(8,128)(2,1)}), bf16[16,64,1024]{2,1,0:T(8,128)(2,1)S(1)}, u32[]{:S(2)}, u32[]{:S(2)}) async-start(bf16[16,64,1024]{2,1,0:T(8,128)(2,1)} %bitcast.8), calls=%async_computation.2 | async-start | bytes 4194304 | tf_op jit(solution)/shard_map/all_to_all | solution.py:56
  43.3 0.0 copy-done.1
  43.3 5.4 %gather_fusion.1 = bf16[1024,1024]{1,0:T(8,128)(2,1)} fusion(bf16[257,1024]{1,0:T(8,128)(2,1)S(1)} %concatenate.20, s32[1024]{0:T(1024)S(1)} %get-tuple-element.25), kind=kCustom, calls=%fused_computation.1 | custom fusion | bytes 4198400 | tf_op jit(solution)/shard_map/gather | solution.py:48
  48.7 23.3 %all-to-all-done.2 = bf16[16,64,1024]{2,1,0:T(8,128)(2,1)S(1)} async-done(((bf16[16,64,1024]{2,1,0:T(8,128)(2,1)}), bf16[16,64,1024]{2,1,0:T(8,128)(2,1)S(1)}, u32[]{:S(2)}, u32[]{:S(2)}) %all-to-all-start.2) | async-done | bytes 2097184 | tf_op jit(solution)/shard_map/all_to_all | solution.py:56
  72.0 5.5 %all-to-all-start.1 = ((bf16[16,64,1024]{2,1,0:T(8,128)(2,1)}), bf16[16,64,1024]{2,1,0:T(8,128)(2,1)}, u32[]{:S(2)}, u32[]{:S(2)}) async-start(bf16[16,64,1024]{2,1,0:T(8,128)(2,1)} %bitcast.4), calls=%async_computation.1 | async-start | bytes 4194304 | tf_op jit(solution)/shard_map/all_to_all | solution.py:57
  77.5 0.2 reduce-scatter.9.cloned.1.call-start
  77.8 0.1 reshape.143
  77.9 16.4 %fusion.4 = f32[16,2,32,2048]{3,2,0,1:T(8,128)} fusion(bf16[1024,2,2048,1]{2,1,0,3:T(2,128)(2,1)} %bitcast.89, bf16[16,2,32,1024]{3,2,1,0:T(8,128)(2,1)S(1)} %bitcast.83), kind=kOutput, calls=%fused_computation.12 | convolution fusion | flops 4294967296 | bytes 18874368 | tf_op jit(solution)/shard_map/secd,def->secf/dot_general | solution.py:63
  94.3 10.7 %all-to-all-done.1 = bf16[16,64,1024]{2,1,0:T(8,128)(2,1)} async-done(((bf16[16,64,1024]{2,1,0:T(8,128)(2,1)}), bf16[16,64,1024]{2,1,0:T(8,128)(2,1)}, u32[]{:S(2)}, u32[]{:S(2)}) %all-to-all-start.1) | async-done | bytes 2097184 | tf_op jit(solution)/shard_map/all_to_all | solution.py:57
  105.0 10.4 %fusion.10 = (bf16[16,2,32,1024]{3,2,0,1:T(8,128)(2,1)}, bf16[16,2,32,1024]{3,2,0,1:T(8,128)(2,1)}, bf16[16,2,32,1024]{3,2,0,1:T(8,128)(2,1)S(1)}) fusion(f32[16,2,32,2048]{3,2,0,1:T(8,128)} %fusion.4, bf16[1024,2,1024,1]{2,1,0,3:T(2,128)(2,1)} %bitcast.91, f32[16,2,32]{2,1,0:T(2,128)S(1)} %reshape.143, bf16[16,64,1024]{2,1,0:T(8,128)(2,1)} %all-to-all-done.1), kind=kOutput, calls=%fused_computation.20 | convolution fusion | flops 2166358016 | bytes 20975616 | tf_op jit(solution)/shard_map/secd,fed->secf/dot_general | solution.py:74
  115.3 0.0 copy-start.2
  115.3 6.8 %bitcast_convert_fusion.1 = bf16[2,1024,1024]{2,1,0:T(8,128)(2,1)} fusion(bf16[16,2,32,1024]{3,2,0,1:T(8,128)(2,1)S(1)} %get-tuple-element.24, f32[16,2,32]{2,1,0:T(2,128)S(1)} %reshape.143, bf16[16,64,1024]{2,1,0:T(8,128)(2,1)} %all-to-all-done.1), kind=kOutput, calls=%fused_computation.7 | convolution fusion | flops 2152726528 | bytes 8392704 | tf_op jit(solution)/shard_map/secf,secd->fed/dot_general | solution.py:19
  122.1 0.0 copy-done.2
  122.1 6.5 %copy.94 = bf16[1024,2048]{1,0:T(8,128)(2,1)} copy(bf16[1024,2048]{0,1:T(8,128)(2,1)} %bitcast.81) | data formatting | bytes 8388608
  128.6 0.0 reduce-scatter.9.cloned.1.call-update
  128.6 0.3 reduce-scatter.7.cloned.1.call-start
  128.9 9.0 %bitcast_convert_fusion = bf16[2,2048,1024]{2,1,0:T(8,128)(2,1)} fusion(bf16[16,2,32,1024]{3,2,0,1:T(8,128)(2,1)} %get-tuple-element.23, bf16[16,2,32,1024]{3,2,0,1:T(8,128)(2,1)} %get-tuple-element.22, bf16[16,2,32,1024]{3,2,1,0:T(8,128)(2,1)S(1)} %bitcast.84), kind=kOutput, calls=%fused_computation.6 | convolution fusion | flops 4307550208 | bytes 14680064 | tf_op jit(solution)/shard_map/secd,secf->def/dot_general | solution.py:11
  137.9 11.3 %copy.92 = bf16[1024,4096]{1,0:T(8,128)(2,1)} copy(bf16[1024,4096]{0,1:T(8,128)(2,1)} %bitcast.78) | data formatting | bytes 16777216
  149.2 0.0 copy-start.3
  149.2 0.0 reduce-scatter.7.cloned.1.call-update
  149.3 1.6 copy-done.3
  150.9 5.6 %fusion.7 = bf16[16,2,32]{2,0,1:T(8,128)(2,1)S(1)} fusion(bf16[16,2,32,1024]{3,2,0,1:T(8,128)(2,1)S(1)} %copy-done.3, bf16[1024,2,1024,1]{2,1,0,3:T(2,128)(2,1)} %bitcast.92, bf16[16,64,1024]{2,1,0:T(8,128)(2,1)} %all-to-all-done.1), kind=kOutput, calls=%fused_computation.15 | convolution fusion | flops 2150628352 | bytes 8390656 | tf_op jit(solution)/shard_map/secf,fed->secd/dot_general | solution.py:69
  156.5 0.7 convert_element_type.109
  157.2 6.3 %all-to-all-start.4 = ((bf16[16,1,64]{2,1,0:T(2,128)(2,1)}), bf16[16,1,64]{2,1,0:T(2,128)(2,1)S(1)}, u32[]{:S(2)}, u32[]{:S(2)}) async-start(bf16[16,1,64]{2,1,0:T(2,128)(2,1)} %convert_element_type.109), calls=%async_computation.4 | async-start | bytes 16384 | tf_op jit(solution)/shard_map/all_to_all | solution.py:88
  163.5 10.7 %convert_bitcast_fusion = bf16[16,2,32,1024]{3,2,0,1:T(8,128)(2,1)S(1)} fusion(bf16[1024,2,2048,1]{2,1,0,3:T(2,128)(2,1)} %bitcast.90, bf16[16,2,32,1024]{3,2,0,1:T(8,128)(2,1)} %get-tuple-element.23, bf16[16,2,32,1024]{3,2,0,1:T(8,128)(2,1)} %get-tuple-element.22), kind=kOutput, calls=%fused_computation.32 | convolution fusion | flops 4304404480 | bytes 14680064 | tf_op jit(solution)/shard_map/secf,def->secd/dot_general | solution.py:77
  174.1 1.5 copy.65
  175.6 0.0 all-to-all-done.4
  175.6 6.7 %all-to-all-start.3 = ((bf16[16,64,1024]{2,1,0:T(8,128)(2,1)}), bf16[16,64,1024]{2,1,0:T(8,128)(2,1)S(1)}, u32[]{:S(2)}, u32[]{:S(2)}) async-start(bf16[16,64,1024]{2,1,0:T(8,128)(2,1)} %bitcast.14), calls=%async_computation.3 | async-start | bytes 4194304 | tf_op jit(solution)/shard_map/all_to_all | solution.py:81
  182.4 0.1 reshape.141
  182.5 3.5 %gather_fusion.4 = bf16[512]{0:T(512)(128)(2,1)S(1)} fusion(bf16[1025]{0:T(1024)(128)(2,1)S(1)} %pad_maximum_fusion.6, s32[1024]{0:T(1024)S(1)} %pad_clamp_fusion), kind=kCustom, calls=%fused_computation.4 | custom fusion | bytes 4096 | tf_op jit(solution)/shard_map/gather | solution.py:102
  186.0 0.2 reshape.142
  186.1 0.7 copy.72
  186.8 23.0 %all-to-all-done.3 = bf16[16,64,1024]{2,1,0:T(8,128)(2,1)S(1)} async-done(((bf16[16,64,1024]{2,1,0:T(8,128)(2,1)}), bf16[16,64,1024]{2,1,0:T(8,128)(2,1)S(1)}, u32[]{:S(2)}, u32[]{:S(2)}) %all-to-all-start.3) | async-done | bytes 2097184 | tf_op jit(solution)/shard_map/all_to_all | solution.py:81
  209.8 0.0 copy-start
  209.8 1.3 copy-done
  211.1 1.8 concatenate.23
  212.9 2.1 gather_fusion.3
  215.0 0.4 gather.21
  215.4 3.6 %reduce_sum.47 = bf16[256,1024]{1,0:T(8,128)(2,1)} reduce(bf16[256,2,1024]{2,1,0:T(2,128)(2,1)S(1)} %gather.21, bf16[]{:T(256)} %constant.38.clone.1), dimensions={1}, to_apply=%region_5.6 | reduce | flops 262144 | bytes 1572866 | tf_op jit(solution)/shard_map/reduce_sum | solution.py:101
  219.0 0.0 reduce-scatter.9.cloned.1.call-done
  219.0 1.3 copy.95
  220.3 1.2 copy.74
  221.5 0.4 reduce-scatter.7.cloned.1.call-done
  221.9 1.6 copy.93
  223.6 2.1 copy.73
  (13 shorter events, 0.2 us)
Async XLA Ops:
  22.4 14.0 %all-to-all-start = ((bf16[16,1,64]{2,1,0:T(2,128)(2,1)}), bf16[16,1,64]{2,1,0:T(2,128)(2,1)S(1)}, u32[]{:S(2)}, u32[]{:S(2)}) async-start(bf16[16,1,64]{2,1,0:T(2,128)(2,1)} %convert_element_type.108), calls=%async_computation | async-start | bytes 16384 | tf_op jit(solution)/shard_map/all_to_all | solution.py:58
  36.5 6.8 %copy-start.1 = (bf16[256,1024]{1,0:T(8,128)(2,1)S(1)}, bf16[256,1024]{1,0:T(8,128)(2,1)}, u32[]{:S(2)}) copy-start(bf16[256,1024]{1,0:T(8,128)(2,1)} %param.8) | copy-start | bytes 1572868
  36.5 35.6 %all-to-all-start.2 = ((bf16[16,64,1024]{2,1,0:T(8,128)(2,1)}), bf16[16,64,1024]{2,1,0:T(8,128)(2,1)S(1)}, u32[]{:S(2)}, u32[]{:S(2)}) async-start(bf16[16,64,1024]{2,1,0:T(8,128)(2,1)} %bitcast.8), calls=%async_computation.2 | async-start | bytes 4194304 | tf_op jit(solution)/shard_map/all_to_all | solution.py:56
  72.0 32.9 %all-to-all-start.1 = ((bf16[16,64,1024]{2,1,0:T(8,128)(2,1)}), bf16[16,64,1024]{2,1,0:T(8,128)(2,1)}, u32[]{:S(2)}, u32[]{:S(2)}) async-start(bf16[16,64,1024]{2,1,0:T(8,128)(2,1)} %bitcast.4), calls=%async_computation.1 | async-start | bytes 4194304 | tf_op jit(solution)/shard_map/all_to_all | solution.py:57
  77.5 141.5 %reduce-scatter.9.cloned.1.call-start = ((), (), s32[]{:S(2)}) async-start(), calls=%async_computation.8 | async-start | bytes 4718592
  115.3 6.8 %copy-start.2 = (bf16[16,2,32,1024]{3,2,0,1:T(8,128)(2,1)}, bf16[16,2,32,1024]{3,2,0,1:T(8,128)(2,1)S(1)}, u32[]{:S(2)}) copy-start(bf16[16,2,32,1024]{3,2,0,1:T(8,128)(2,1)S(1)} %get-tuple-element.24) | copy-start | bytes 6291460
  128.6 93.3 %reduce-scatter.7.cloned.1.call-start = ((), (), s32[]{:S(2)}) async-start(), calls=%async_computation.7 | async-start | bytes 9437184
  149.2 1.6 copy-start.3
  157.2 18.5 %all-to-all-start.4 = ((bf16[16,1,64]{2,1,0:T(2,128)(2,1)}), bf16[16,1,64]{2,1,0:T(2,128)(2,1)S(1)}, u32[]{:S(2)}, u32[]{:S(2)}) async-start(bf16[16,1,64]{2,1,0:T(2,128)(2,1)} %convert_element_type.109), calls=%async_computation.4 | async-start | bytes 16384 | tf_op jit(solution)/shard_map/all_to_all | solution.py:88
  175.6 34.2 %all-to-all-start.3 = ((bf16[16,64,1024]{2,1,0:T(8,128)(2,1)}), bf16[16,64,1024]{2,1,0:T(8,128)(2,1)S(1)}, u32[]{:S(2)}, u32[]{:S(2)}) async-start(bf16[16,64,1024]{2,1,0:T(8,128)(2,1)} %bitcast.14), calls=%async_computation.3 | async-start | bytes 4194304 | tf_op jit(solution)/shard_map/all_to_all | solution.py:81
  209.8 1.3 copy-start
Sparse Core Ops, SparseCore 0:
  128.7 36.9 reduce-scatter.8
  168.1 53.7 reduce-scatter.6
where the time goes:
time: 236 us; the launch traced here: 233 us
  local copies, waits for them, and re-layouts  62.3 us (26%)
  matrix products  58.8 us (25%)
  waiting for transfers between devices  57.4 us (24%)
  starting transfers between devices  33.3 us (14%)
  between operations  14.3 us (6%)
  other arithmetic  6.36 us (3%)
    unnamed x17, local copies, waits for them, and re-layouts  29.2 us
    all_to_all x1, waiting for transfers between devices, on_device(): lax.all_to_all(send_x, 'expert', split_axis=0, concat_axis=0, tiled=True)  23.3 us
    all_to_all x1, waiting for transfers between devices, on_device(): lax.all_to_all(slot_grad.reshape(peers, exp_local * slots, model_width),...  23 us
    dot_general x1, matrix products, on_device(): jnp.einsum('secd,def->secf', slot_x, weight_in, preferred_element_type=jn...  16.4 us
    all_to_all x1, waiting for transfers between devices, on_device(): lax.all_to_all(send_dy, 'expert', split_axis=0, concat_axis=0, tiled=True)  10.7 us
    dot_general x1, matrix products, on_device(): jnp.einsum('secf,def->secd', dpre, weight_in, preferred_element_type=jnp....  10.7 us
    dot_general x1, matrix products, on_device(): jnp.einsum('secd,fed->secf', scaled, weight_down, preferred_element_type=...  10.4 us
    dot_general x1, matrix products, weight_sums(): jnp.einsum('secd,secf->def', slot_x, dpre, preferred_element_type=jnp.flo...  9.04 us
  transfers between devices with their start and end apart: 7, of which 4 were waited for; matrix products, arithmetic and copies ran while one was open for 35% of the time, Pallas kernels for 0%

commit v1 on v0

v1 whole, which is shorter than its diff:
```python
import jax
import jax.numpy as jnp
from jax import lax
from jax.experimental import pallas as pl
from jax.experimental.pallas import tpu as pltpu
from jax.sharding import PartitionSpec as P

MESH = pl.DeviceIdType.MESH
BF16 = jnp.bfloat16
F32 = jnp.float32

D = 1024
FF = 1024
TOK = 256
CAP = 32
EXPERTS = 32
LOCAL = 2
PEERS = 16
SLOTS = PEERS * CAP
WIDE = 2 * FF + FF
HALF = 128
TILE = 256
RET = D + 128
STAGE = 128

PARTNERS = (
    (0, 0), (1, 0), (3, 0), (0, 1), (0, 3), (1, 1), (3, 3), (2, 2),
    (1, 3), (3, 1), (2, 0), (0, 2), (1, 2), (3, 2), (2, 1), (2, 3),
)
STEPS = (2, 1, 3, 0)


def dot(a, b):
    return lax.dot_general(a, b, (((1,), (0,)), ((), ())), preferred_element_type=F32)


def dot_nt(a, b):
    return lax.dot_general(a, b, (((1,), (1,)), ((), ())), preferred_element_type=F32)


def dot_tn(a, b):
    return lax.dot_general(a, b, (((0,), (0,)), ((), ())), preferred_element_type=F32)


def kernel(
    tokens, cotangent, combine, ids, capacity, w_in, w_down,
    token_out, combine_out, inner_out, down_out,
    raw_in, raw_down, win, wdown, pick0, pick1, send, recv, hidden, dpre, turned,
    part, core_sum, relay, arrived, ret_send, ret_recv,
    raw_sem, send_sem, recv_sem, ret_send_sem, ret_recv_sem,
    core_send_sem, core_recv_sem, z_send_sem, z_recv_sem,
):
    dp = lax.axis_index("dp")
    ex = lax.axis_index("expert")
    z, core = dp // 2, dp % 2
    y, x = ex // 4, ex % 4

    def partner(i, sign):
        dx, dy = PARTNERS[i]
        return ((y + 4 + sign * dy) % 4) * 4 + (x + 4 + sign * dx) % 4

    def along_z(step):
        return (((z + step) % 4) * 2 + core, ex)

    sibling = (z * 2 + 1 - core, ex)

    def dispatch(e, i):
        return pltpu.make_async_remote_copy(
            src_ref=send.at[e, i], dst_ref=recv.at[e, i],
            send_sem=send_sem.at[e, i], recv_sem=recv_sem.at[e, i],
            device_id=(dp, partner(i, 1)), device_id_type=MESH,
        )

    def give_back(e, i):
        return pltpu.make_async_remote_copy(
            src_ref=ret_send.at[e, i], dst_ref=ret_recv.at[e, i],
            send_sem=ret_send_sem.at[e, i], recv_sem=ret_recv_sem.at[e, i],
            device_id=(dp, partner(i, -1)), device_id_type=MESH,
        )

    def to_sibling(e, s):
        return pltpu.make_async_remote_copy(
            src_ref=part.at[s, 1 - core], dst_ref=core_sum.at[e, s],
            send_sem=core_send_sem.at[e, s], recv_sem=core_recv_sem.at[e, s],
            device_id=sibling, device_id_type=MESH,
        )

    half = HALF // 2

    def z_copy(e, k):
        src, dst, step = (
            (core_sum.at[e, 0, pl.ds(0, half)], relay.at[e, 0], 1),
            (core_sum.at[e, 0, pl.ds(half, half)], relay.at[e, 1], 3),
            (core_sum.at[e, 1, pl.ds(half, half)], arrived.at[e, 0, pl.ds(half, half)], 1),
            (core_sum.at[e, 2, pl.ds(0, half)], arrived.at[e, 1, pl.ds(0, half)], 3),
            (core_sum.at[e, 1, pl.ds(0, half)], arrived.at[e, 0, pl.ds(0, half)], 1),
            (core_sum.at[e, 2, pl.ds(half, half)], arrived.at[e, 1, pl.ds(half, half)], 3),
        )[k]
        return pltpu.make_async_remote_copy(
            src_ref=src, dst_ref=dst, send_sem=z_send_sem.at[e, k], recv_sem=z_recv_sem.at[e, k],
            device_id=along_z(step), device_id_type=MESH,
        )

    def raw_copy(j, slot, which):
        src, dst = ((w_in, raw_in), (w_down, raw_down))[which]
        return pltpu.make_async_copy(
            src.at[pl.ds(pl.multiple_of(j * STAGE, STAGE), STAGE)], dst.at[slot],
            raw_sem.at[which, slot],
        )

    for which in (0, 1):
        raw_copy(0, 0, which).start()

    barrier = pltpu.get_barrier_semaphore()
    greeted = [(dp, partner(i, 1)) for i in range(1, PEERS)] + [sibling, along_z(1), along_z(3)]
    for device in greeted:
        pl.semaphore_signal(barrier, inc=1, device_id=device, device_id_type=MESH)

    rows = lax.broadcasted_iota(jnp.int32, (TOK, TOK), 0)
    columns = lax.broadcasted_iota(jnp.int32, (TOK, TOK), 1)
    earlier = (columns < rows).astype(F32).astype(BF16)
    lane = lax.broadcasted_iota(jnp.int32, (TOK, EXPERTS), 1)
    id0, id1 = ids[:, 0:1], ids[:, 1:2]
    named0 = (id0 == lane).astype(F32)
    named1 = (id1 == lane).astype(F32)
    before = dot(earlier, (named0 + named1).astype(BF16))
    limits = capacity[...].astype(F32)

    def target(named, number):
        position = jnp.sum(named * before, axis=1, keepdims=True)
        limit = jnp.sum(named * limits, axis=1, keepdims=True)
        return jnp.where(position < limit, number * CAP + position.astype(jnp.int32), -1)

    target0, target1 = target(named0, id0), target(named1, id1)
    slot_lane = lax.broadcasted_iota(jnp.int32, (1, SLOTS), 1)
    first = jnp.zeros((1, SLOTS), jnp.int32)
    for i in range(PEERS):
        first = jnp.where(slot_lane // CAP == i, partner(i, 1) * (LOCAL * CAP), first)
    first = first + slot_lane % CAP
    for e in range(LOCAL):
        wanted = first + e * CAP
        pick0[e] = (target0 == wanted).astype(F32).astype(BF16)
        pick1[e] = (target1 == wanted).astype(F32).astype(BF16)

    cb0 = combine[:, 0:1].astype(BF16).astype(F32)
    cb1 = combine[:, 1:2].astype(BF16).astype(F32)

    def gather(e, group):
        lanes = pl.ds(group * 128, 128)
        p0, p1 = pick0[e, :, lanes], pick1[e, :, lanes]
        for c in range(0, D, TILE):
            cols = pl.ds(c, TILE)
            cot = cotangent[:, cols].astype(F32)
            rows_x = dot_tn(p0 + p1, tokens[:, cols]).astype(BF16)
            rows_s = (
                dot_tn(p0, (cb0 * cot).astype(BF16)) + dot_tn(p1, (cb1 * cot).astype(BF16))
            ).astype(BF16)
            for j in range(4):
                i = group * 4 + j
                buffer = recv if i == 0 else send
                buffer[e, i, 0:CAP, cols] = rows_x[j * CAP:(j + 1) * CAP]
                buffer[e, i, CAP:2 * CAP, cols] = rows_s[j * CAP:(j + 1) * CAP]

    def start_dispatch(e, lo, hi):
        for i in range(max(lo, 1), hi):
            dispatch(e, i).start()

    for group in range(4):
        gather(0, group)
        if group == 0:
            pl.semaphore_wait(barrier, len(greeted))
        start_dispatch(0, group * 4, group * 4 + 4)
    for group in range(4):
        gather(1, group)

    def settle(j, _):
        slot = j % 2

        @pl.when(j + 1 < D // STAGE)
        def _():
            for which in (0, 1):
                raw_copy(j + 1, 1 - slot, which).start()

        for which in (0, 1):
            raw_copy(j, slot, which).wait()

        def block(b, _):
            src = pl.multiple_of(b * 16, 16)
            dst = pl.ds(pl.multiple_of(j * STAGE + b * 16, 16), 16)
            win[:, dst, :] = jnp.swapaxes(raw_in[slot, pl.ds(src, 16)], 0, 1)
            wdown[:, dst, :] = jnp.swapaxes(raw_down[slot, pl.ds(src, 16)], 0, 1)
            return 0

        lax.fori_loop(0, STAGE // 16, block, 0)
        return 0

    lax.fori_loop(0, D // STAGE, settle, 0)

    def arrive(e, lo, hi):
        for i in range(max(lo, 1), hi):
            dispatch(e, i).wait_recv()

    def rows_of(e, h, lo, cols):
        return recv[e, h * 8:h * 8 + 8, lo:lo + CAP, cols].reshape(8 * CAP, -1)

    def forward(e, h):
        here = pl.ds(h * 256, 256)

        def tile(n, total):
            at = pl.multiple_of(n * TILE, TILE)
            cols, upper = pl.ds(at, TILE), pl.ds(FF + at, TILE)
            xs = rows_of(e, h, 0, slice(None))
            gate = dot(xs, win[e, :, cols])
            up = dot(xs, win[e, :, upper])
            dh = dot_nt(rows_of(e, h, CAP, slice(None)), wdown[e, cols, :])
            sig = jax.nn.sigmoid(gate)
            act = gate * sig
            hid = (act * up).astype(BF16)
            hidden[here, cols] = hid
            dpre[here, cols] = (dh * up * sig * (1.0 + gate * (1.0 - sig))).astype(BF16)
            dpre[here, upper] = (dh * act).astype(BF16)
            return total + jnp.sum(hid.astype(F32) * dh, axis=1, keepdims=True)

        total = lax.fori_loop(0, FF // TILE, tile, jnp.zeros((256, 1), F32))
        total = jnp.broadcast_to(total.astype(BF16), (256, 128)).reshape(8, CAP, 128)
        for j in range(8):
            i = h * 8 + j
            buffer = ret_recv if i == 0 else ret_send
            buffer[e, i, :, D:RET] = total[j]

    def partial(e, s):
        at = pl.multiple_of(((z + STEPS[s]) % 4) * TILE, TILE)
        turned[...] = recv[e, :, 0:CAP, pl.ds(at, TILE)].reshape(SLOTS, TILE).T

        def inner_tile(n, _):
            cols = pl.ds(pl.multiple_of(n * TILE, TILE), TILE)
            part[s, :, :, cols] = dot(turned[...], dpre[:, cols]).astype(BF16).reshape(2, HALF, TILE)
            return 0

        lax.fori_loop(0, 2 * FF // TILE, inner_tile, 0)
        turned[...] = hidden[:, pl.ds(at, TILE)].T

        def down_tile(n, _):
            at = pl.multiple_of(n * TILE, TILE)
            scaled = recv[e, :, CAP:2 * CAP, pl.ds(at, TILE)].reshape(SLOTS, TILE)
            part[s, :, :, pl.ds(2 * FF + at, TILE)] = (
                dot(turned[...], scaled).astype(BF16).reshape(2, HALF, TILE)
            )
            return 0

        lax.fori_loop(0, D // TILE, down_tile, 0)

    def add_rows(dst, lo, count, other):
        def block(b, _):
            at = pl.multiple_of(b * 16, 16)
            here = dst[pl.ds(lo + at, 16)].astype(F32)
            dst[pl.ds(lo + at, 16)] = (here + other[pl.ds(at, 16)].astype(F32)).astype(BF16)
            return 0

        lax.fori_loop(0, count // 16, block, 0)

    def meet_sibling(e, s):
        to_sibling(e, s).wait_recv()
        add_rows(core_sum.at[e, s], 0, HALF, part.at[s, core])
        for k in ((0, 1), (2,), (3,), ())[s]:
            z_copy(e, k).start()

    def weight_sums(e):
        for s in range(4):
            partial(e, s)
            to_sibling(e, s).start()
            if s > 0:
                meet_sibling(e, s - 1)
        meet_sibling(e, 3)

    def pass_on(e):
        z_copy(e, 0).wait_recv()
        add_rows(core_sum.at[e, 1], 0, half, relay.at[e, 0])
        z_copy(e, 4).start()
        z_copy(e, 1).wait_recv()
        add_rows(core_sum.at[e, 2], half, half, relay.at[e, 1])
        z_copy(e, 5).start()

    def input_grad(e, h):
        def tile(n, _):
            cols = pl.ds(pl.multiple_of(n * TILE, TILE), TILE)
            grad = dot_nt(dpre[pl.ds(h * 256, 256), :], win[e, cols, :]).astype(BF16)
            grad = grad.reshape(8, CAP, TILE)
            for j in range(8):
                i = h * 8 + j
                buffer = ret_recv if i == 0 else ret_send
                buffer[e, i, :, cols] = grad[j]
            return 0

        lax.fori_loop(0, D // TILE, tile, 0)
        for i in range(max(h * 8, 1), h * 8 + 8):
            give_back(e, i).start()

    def finish_sums(e):
        for k in (2, 3, 4, 5):
            z_copy(e, k).wait_recv()

        def block(b, _):
            at = pl.ds(pl.multiple_of(b * 16, 16), 16)
            total = core_sum[e, 3, at].astype(F32)
            total = total + arrived[e, 0, at].astype(F32) + arrived[e, 1, at].astype(F32)
            inner_out[e, at, :] = total[:, :2 * FF]
            down_out[e, at, :] = total[:, 2 * FF:]
            return 0

        lax.fori_loop(0, HALF // 16, block, 0)

    for e in range(LOCAL):
        arrive(e, 0, 8)
        if e == 0:
            start_dispatch(1, 0, PEERS)
        forward(e, 0)
        arrive(e, 8, PEERS)
        forward(e, 1)
        if e == 1:
            for s in range(4):
                to_sibling(0, s).wait_send()
        weight_sums(e)
        input_grad(e, 0)
        pass_on(e)
        input_grad(e, 1)

    finish_sums(0)

    for e in range(LOCAL):
        for i in range(1, PEERS):
            give_back(e, i).wait_recv()
    for c in range(0, D, TILE):
        cols = pl.ds(c, TILE)
        total = jnp.zeros((TOK, TILE), F32)
        for e in range(LOCAL):
            total = total + dot(
                pick0[e] + pick1[e], ret_recv[e, :, :, cols].reshape(SLOTS, TILE)
            )
        token_out[:, cols] = total.astype(BF16)
    for k, (pick, cb) in enumerate(((pick0, cb0), (pick1, cb1))):
        total = jnp.zeros((TOK, 128), F32)
        for e in range(LOCAL):
            total = total + dot(pick[e], ret_recv[e, :, :, D:RET].reshape(SLOTS, 128))
        combine_out[:, k:k + 1] = (total[:, 0:1] / cb).astype(BF16)

    finish_sums(1)

    for e in range(LOCAL):
        for i in range(1, PEERS):
            dispatch(e, i).wait_send()
            give_back(e, i).wait_send()
        for k in range(6):
            z_copy(e, k).wait_send()
    for s in range(4):
        to_sibling(1, s).wait_send()


def on_device(tokens, cotangent, combine, expert_ids, capacity, weight_in, weight_down):
    vmem = pl.BlockSpec(memory_space=pltpu.VMEM)
    hbm = pl.BlockSpec(memory_space=pl.ANY)
    token_grad, combine_grad, inner, down = pl.pallas_call(
        kernel,
        out_shape=(
            jax.ShapeDtypeStruct((TOK, D), BF16),
            jax.ShapeDtypeStruct((TOK, 2), BF16),
            jax.ShapeDtypeStruct((LOCAL, HALF, 2 * FF), F32),
            jax.ShapeDtypeStruct((LOCAL, HALF, D), F32),
        ),
        in_specs=[vmem] * 5 + [hbm] * 2,
        out_specs=(vmem,) * 4,
        scratch_shapes=[
            pltpu.VMEM((2, STAGE, LOCAL, 2 * FF), BF16),
            pltpu.VMEM((2, STAGE, LOCAL, D), BF16),
            pltpu.VMEM((LOCAL, D, 2 * FF), BF16),
            pltpu.VMEM((LOCAL, FF, D), BF16),
            pltpu.VMEM((LOCAL, TOK, SLOTS), BF16),
            pltpu.VMEM((LOCAL, TOK, SLOTS), BF16),
            pltpu.VMEM((LOCAL, PEERS, 2 * CAP, D), BF16),
            pltpu.VMEM((LOCAL, PEERS, 2 * CAP, D), BF16),
            pltpu.VMEM((SLOTS, FF), BF16),
            pltpu.VMEM((SLOTS, 2 * FF), BF16),
            pltpu.VMEM((TILE, SLOTS), BF16),
            pltpu.VMEM((4, 2, HALF, WIDE), BF16),
            pltpu.VMEM((LOCAL, 4, HALF, WIDE), BF16),
            pltpu.VMEM((LOCAL, 2, HALF // 2, WIDE), BF16),
            pltpu.VMEM((LOCAL, 2, HALF, WIDE), BF16),
            pltpu.VMEM((LOCAL, PEERS, CAP, RET), BF16),
            pltpu.VMEM((LOCAL, PEERS, CAP, RET), BF16),
            pltpu.SemaphoreType.DMA((2, 2)),
            pltpu.SemaphoreType.DMA((LOCAL, PEERS)),
            pltpu.SemaphoreType.DMA((LOCAL, PEERS)),
            pltpu.SemaphoreType.DMA((LOCAL, PEERS)),
            pltpu.SemaphoreType.DMA((LOCAL, PEERS)),
            pltpu.SemaphoreType.DMA((LOCAL, 4)),
            pltpu.SemaphoreType.DMA((LOCAL, 4)),
            pltpu.SemaphoreType.DMA((LOCAL, 6)),
            pltpu.SemaphoreType.DMA((LOCAL, 6)),
        ],
        compiler_params=pltpu.CompilerParams(
            collective_id=0, has_side_effects=True, vmem_limit_bytes=62 * 2**20
        ),
        name="moe_backward",
    )(tokens, cotangent, combine, expert_ids, capacity.reshape(1, EXPERTS), weight_in, weight_down)
    return (
        token_grad,
        combine_grad,
        jnp.transpose(inner, (1, 0, 2)),
        jnp.transpose(down, (1, 0, 2)),
    )


def solution(mesh):
    placed = (
        P(("dp", "expert"), None),
        P(("dp", "expert"), None),
        P(("dp", "expert"), None),
        P(("dp", "expert"), None),
        P(),
        P(None, "expert", None),
        P(None, "expert", None),
    )
    return jax.shard_map(
        on_device,
        mesh=mesh,
        in_specs=placed,
        out_specs=(
            P(("dp", "expert"), None),
            P(("dp", "expert"), None),
            P("dp", "expert", None),
            P("dp", "expert", None),
        ),
        check_vma=False,
    )
```

time: 236 us -> 118 us (0.50); the launches traced: 233 us -> 118 us
  Pallas kernels: 0 us -> 104 us
  matrix products: 58.8 us -> 0 us
  waiting for transfers between devices: 57.4 us -> 0 us
  local copies, waits for them, and re-layouts: 62.3 us -> 12.8 us
  starting transfers between devices: 33.3 us -> 0 us
  between operations: 14.3 us -> 0.65 us
  other arithmetic: 6.36 us -> 0 us
    pallas_call x0 -> x1, Pallas kernels: none -> 104 us  [on_device(): pl.pallas_call(kernel, out_shape=(jax.ShapeDtypeStruct((TOK, D), BF16), j...]
    dot_general x6 -> x0, matrix products: 58.8 us -> none  [the longest x1 16.4 us: on_device(): jnp.einsum('secd,def->secf', slot_x, weight_in, preferred_element_type=jn...]
    all_to_all x5 -> x0, waiting for transfers between devices: 57 us -> none  [the longest x1 23.3 us: on_device(): lax.all_to_all(send_x, 'expert', split_axis=0, concat_axis=0, tiled=True)]
    all_to_all x5 -> x0, starting transfers between devices: 32.8 us -> none  [the longest x1 7.58 us: on_device(): lax.all_to_all(send_c, 'expert', split_axis=0, concat_axis=0, tiled=True)]
    gather x6 -> x0, local copies, waits for them, and re-layouts: 23.5 us -> none  [the longest x1 6.8 us: on_device(): jnp.concatenate([combine.reshape(-1), jnp.zeros((1,), jnp.float32)], axis=0)]
    unnamed x17 -> x8, local copies, waits for them, and re-layouts: 29.2 us -> 12.8 us
    reduce_sum x2 -> x0, other arithmetic: 4.35 us -> none  [the longest x1 3.59 us: on_device(): token_grad = jnp.sum(per_assign, axis=1).astype(jnp.bfloat16)]
    convert_element_type x5 -> x0, local copies, waits for them, and re-layouts: 2.94 us -> none  [the longest x1 1.49 us: on_device(): slot_grad = jnp.einsum('secf,def->secd', dpre, weight_in, preferred_eleme...]
  transfers between devices with their start and end apart: 7 -> 0, of which waited for: 4 -> 0; matrix products, arithmetic and copies ran while one was open for 35% -> 0% of each run, Pallas kernels for 0% -> 0%
where the time goes in v1:
time: 118 us
  Pallas kernels  104 us (88%)
  local copies, waits for them, and re-layouts  12.8 us (11%)
    pallas_call x1, Pallas kernels, on_device(): pl.pallas_call(kernel, out_shape=(jax.ShapeDtypeStruct((TOK, D), BF16), j...  104 us
    unnamed x8, local copies, waits for them, and re-layouts  12.8 us

profile of v1, /device:TPU:1, one launch (start us, length us, event | category | flops | bytes accessed | tf_op | source)
XLA Modules:
  0.0 117.9 jit_solution(9071219023276294181)
XLA Ops:
  0.6 1.5 %copy.11.combine = f32[256,2]{1,0:T(8,128)} copy(f32[256,2]{0,1:T(2,128)} %param.9) | data formatting | bytes 4096 | tf_op args[2]
  2.1 1.5 %copy.12.ids = s32[256,2]{1,0:T(8,128)} copy(s32[256,2]{0,1:T(2,128)} %param.10) | data formatting | bytes 4096 | tf_op args[3]
  3.6 104.5 %moe_backward.1 = (bf16[256,1024]{1,0:T(8,128)(2,1)}, bf16[256,2]{1,0:T(8,128)(2,1)}, f32[2,128,2048]{2,1,0:T(8,128)}, f32[2,128,1024]{2,1,0:T(8,128)}) custom-call(bf16[256,1024]{1,0:T(8,128)(2,1)} %tokens.1, bf16[256,1024]{1,0:T(8,128)(2,1)} %cotangent.1, f32[256,2]{1,0:T(8,128)} %copy.11.combine, s32[256,2]{1,0:T(8,128)} %copy.12.ids, s32[1,32]{1,0:T(1,128)} %bitcast.5, ...), custom_call_target="tpu_custom_call" | custom-call | tf_op jit(solution)/shard_map/moe_backward/pallas_call | solution.py:362
  108.1 0.0 copy-start
  108.1 1.5 %copy.13 = bf16[256,2]{0,1:T(2,128)(2,1)} copy(bf16[256,2]{1,0:T(8,128)(2,1)} %get-tuple-element.13) | data formatting | bytes 2048
  109.6 3.0 %copy.15 = f32[128,2,1024]{2,1,0:T(2,128)} copy(f32[128,2,1024]{2,0,1:T(8,128)} %bitcast.4) | data formatting | bytes 2097152
  112.6 4.5 %copy.14 = f32[128,2,2048]{2,1,0:T(2,128)} copy(f32[128,2,2048]{2,0,1:T(8,128)} %bitcast.3) | data formatting | bytes 4194304
  117.1 0.0 copy-done
  117.1 0.8 copy.17
Async XLA Ops:
  108.1 9.1 %copy-start = (bf16[256,1024]{1,0:T(8,128)(2,1)S(1)}, bf16[256,1024]{1,0:T(8,128)(2,1)}, u32[]{:S(2)}) copy-start(bf16[256,1024]{1,0:T(8,128)(2,1)} %get-tuple-element.20) | copy-start | bytes 1572868

commit v2 on v1

--- a/solution.py
+++ b/solution.py
@@ -22,6 +22,7 @@
 TILE = 256
 RET = D + 128
 STAGE = 128
+PARTS = 4
 
 PARTNERS = (
     (0, 0), (1, 0), (3, 0), (0, 1), (0, 3), (1, 1), (3, 3), (2, 2),
@@ -43,12 +44,13 @@
 
 
 def kernel(
-    tokens, cotangent, combine, ids, capacity, w_in, w_down,
-    token_out, combine_out, inner_out, down_out,
+    tokens_in, cotangent_in, combine_in, ids_in, capacity_in, w_in, w_down,
+    token_out, combine_out, own, arrived,
+    tokens, cotangent, combine, ids, capacity,
     raw_in, raw_down, win, wdown, pick0, pick1, send, recv, hidden, dpre, turned,
-    part, core_sum, relay, arrived, ret_send, ret_recv,
-    raw_sem, send_sem, recv_sem, ret_send_sem, ret_recv_sem,
-    core_send_sem, core_recv_sem, z_send_sem, z_recv_sem,
+    part, core_sum, relay, ret_send, ret_recv,
+    in_sem, raw_sem, send_sem, recv_sem, ret_send_sem, ret_recv_sem,
+    core_send_sem, core_recv_sem, z_send_sem, z_recv_sem, keep_sem,
 ):
     dp = lax.axis_index("dp")
     ex = lax.axis_index("expert")
@@ -101,6 +103,9 @@
             device_id=along_z(step), device_id_type=MESH,
         )
 
+    def keep(e):
+        return pltpu.make_async_copy(core_sum.at[e, 3], own.at[e], keep_sem.at[e])
+
     def raw_copy(j, slot, which):
         src, dst = ((w_in, raw_in), (w_down, raw_down))[which]
         return pltpu.make_async_copy(
@@ -108,19 +113,34 @@
             raw_sem.at[which, slot],
         )
 
-    for which in (0, 1):
-        raw_copy(0, 0, which).start()
-
     barrier = pltpu.get_barrier_semaphore()
     greeted = [(dp, partner(i, 1)) for i in range(1, PEERS)] + [sibling, along_z(1), along_z(3)]
     for device in greeted:
         pl.semaphore_signal(barrier, inc=1, device_id=device, device_id_type=MESH)
 
+    fetched = [
+        pltpu.make_async_copy(src, dst, in_sem.at[n])
+        for n, (src, dst) in enumerate((
+            (ids_in, ids), (capacity_in, capacity), (combine_in, combine),
+            (tokens_in, tokens), (cotangent_in, cotangent),
+        ))
+    ]
+    for copy in fetched:
+        copy.start()
+    for which in (0, 1):
+        raw_copy(0, 0, which).start()
+    for copy in fetched[:3]:
+        copy.wait()
+
     rows = lax.broadcasted_iota(jnp.int32, (TOK, TOK), 0)
     columns = lax.broadcasted_iota(jnp.int32, (TOK, TOK), 1)
     earlier = (columns < rows).astype(F32).astype(BF16)
     lane = lax.broadcasted_iota(jnp.int32, (TOK, EXPERTS), 1)
-    id0, id1 = ids[:, 0:1], ids[:, 1:2]
+    stood = jnp.concatenate(
+        [ids[...].astype(F32), combine[...].astype(BF16).astype(F32), jnp.zeros((4, TOK), F32)], axis=0
+    ).T
+    id0, id1 = stood[:, 0:1].astype(jnp.int32), stood[:, 1:2].astype(jnp.int32)
+    cb0, cb1 = stood[:, 2:3], stood[:, 3:4]
     named0 = (id0 == lane).astype(F32)
     named1 = (id1 == lane).astype(F32)
     before = dot(earlier, (named0 + named1).astype(BF16))
@@ -141,9 +161,6 @@
         wanted = first + e * CAP
         pick0[e] = (target0 == wanted).astype(F32).astype(BF16)
         pick1[e] = (target1 == wanted).astype(F32).astype(BF16)
-
-    cb0 = combine[:, 0:1].astype(BF16).astype(F32)
-    cb1 = combine[:, 1:2].astype(BF16).astype(F32)
 
     def gather(e, group):
         lanes = pl.ds(group * 128, 128)
@@ -165,6 +182,8 @@
         for i in range(max(lo, 1), hi):
             dispatch(e, i).start()
 
+    for copy in fetched[3:]:
+        copy.wait()
     for group in range(4):
         gather(0, group)
         if group == 0:
@@ -221,7 +240,7 @@
             dpre[here, upper] = (dh * act).astype(BF16)
             return total + jnp.sum(hid.astype(F32) * dh, axis=1, keepdims=True)
 
-        total = lax.fori_loop(0, FF // TILE, tile, jnp.zeros((256, 1), F32))
+        total = lax.fori_loop(0, FF // TILE, tile, jnp.zeros((256, 1), F32), unroll=True)
         total = jnp.broadcast_to(total.astype(BF16), (256, 128)).reshape(8, CAP, 128)
         for j in range(8):
             i = h * 8 + j
@@ -237,7 +256,7 @@
             part[s, :, :, cols] = dot(turned[...], dpre[:, cols]).astype(BF16).reshape(2, HALF, TILE)
             return 0
 
-        lax.fori_loop(0, 2 * FF // TILE, inner_tile, 0)
+        lax.fori_loop(0, 2 * FF // TILE, inner_tile, 0, unroll=True)
         turned[...] = hidden[:, pl.ds(at, TILE)].T
 
         def down_tile(n, _):
@@ -248,7 +267,7 @@
             )
             return 0
 
-        lax.fori_loop(0, D // TILE, down_tile, 0)
+        lax.fori_loop(0, D // TILE, down_tile, 0, unroll=True)
 
     def add_rows(dst, lo, count, other):
         def block(b, _):
@@ -272,6 +291,7 @@
             if s > 0:
                 meet_sibling(e, s - 1)
         meet_sibling(e, 3)
+        keep(e).start()
 
     def pass_on(e):
         z_copy(e, 0).wait_recv()
@@ -292,23 +312,9 @@
                 buffer[e, i, :, cols] = grad[j]
             return 0
 
-        lax.fori_loop(0, D // TILE, tile, 0)
+        lax.fori_loop(0, D // TILE, tile, 0, unroll=True)
         for i in range(max(h * 8, 1), h * 8 + 8):
             give_back(e, i).start()
-
-    def finish_sums(e):
-        for k in (2, 3, 4, 5):
-            z_copy(e, k).wait_recv()
-
-        def block(b, _):
-            at = pl.ds(pl.multiple_of(b * 16, 16), 16)
-            total = core_sum[e, 3, at].astype(F32)
-            total = total + arrived[e, 0, at].astype(F32) + arrived[e, 1, at].astype(F32)
-            inner_out[e, at, :] = total[:, :2 * FF]
-            down_out[e, at, :] = total[:, 2 * FF:]
-            return 0
-
-        lax.fori_loop(0, HALF // 16, block, 0)
 
     for e in range(LOCAL):
         arrive(e, 0, 8)
@@ -325,8 +331,6 @@
         pass_on(e)
         input_grad(e, 1)
 
-    finish_sums(0)
-
     for e in range(LOCAL):
         for i in range(1, PEERS):
             give_back(e, i).wait_recv()
@@ -338,13 +342,14 @@
                 pick0[e] + pick1[e], ret_recv[e, :, :, cols].reshape(SLOTS, TILE)
             )
         token_out[:, cols] = total.astype(BF16)
-    for k, (pick, cb) in enumerate(((pick0, cb0), (pick1, cb1))):
+    router = []
+    for pick, cb in ((pick0, cb0), (pick1, cb1)):
         total = jnp.zeros((TOK, 128), F32)
         for e in range(LOCAL):
             total = total + dot(pick[e], ret_recv[e, :, :, D:RET].reshape(SLOTS, 128))
-        combine_out[:, k:k + 1] = (total[:, 0:1] / cb).astype(BF16)
-
-    finish_sums(1)
+        router.append(total[:, 0:1] / cb)
+    router = jnp.concatenate(router + [jnp.zeros((TOK, 6), F32)], axis=1)
+    combine_out[...] = router.T[0:2].astype(BF16)
 
     for e in range(LOCAL):
         for i in range(1, PEERS):
@@ -352,24 +357,83 @@
             give_back(e, i).wait_send()
         for k in range(6):
             z_copy(e, k).wait_send()
+        for k in (2, 3, 4, 5):
+            z_copy(e, k).wait_recv()
+        keep(e).wait()
     for s in range(4):
         to_sibling(1, s).wait_send()
+
+
+def finish(
+    token_in, combine_in, own_in, arrived_in, token_out, combine_out, inner_out, down_out,
+    token, own, arrived, inner, down, token_sem, in_sem, out_sem,
+):
+    rows = HALF // PARTS
+    fetched = pltpu.make_async_copy(token_in, token, token_sem.at[0])
+    passed = pltpu.make_async_copy(token, token_out, token_sem.at[1])
+    fetched.start()
+
+    def load(p):
+        here = pl.ds(p * rows, rows)
+        return (
+            pltpu.make_async_copy(own_in.at[:, here], own.at[:, here], in_sem.at[0, p]),
+            pltpu.make_async_copy(arrived_in.at[:, :, here], arrived.at[:, :, here], in_sem.at[1, p]),
+        )
+
+    def store(p):
+        here = pl.ds(p * rows, rows)
+        return (
+            pltpu.make_async_copy(inner.at[here], inner_out.at[here], out_sem.at[0, p]),
+            pltpu.make_async_copy(down.at[here], down_out.at[here], out_sem.at[1, p]),
+        )
+
+    for p in range(PARTS):
+        for copy in load(p):
+            copy.start()
+    combine_out[...] = combine_in[...]
+    fetched.wait()
+    passed.start()
+    for p in range(PARTS):
+        for copy in load(p):
+            copy.wait()
+
+        def block(b, _):
+            at = pl.ds(pl.multiple_of(p * rows + b * 16, 16), 16)
+            total = own[:, at].astype(F32)
+            total = total + arrived[:, 0, at].astype(F32) + arrived[:, 1, at].astype(F32)
+            total = jnp.swapaxes(total, 0, 1)
+            inner[at] = total[..., :2 * FF]
+            down[at] = total[..., 2 * FF:]
+            return 0
+
+        lax.fori_loop(0, rows // 16, block, 0)
+        for copy in store(p):
+            copy.start()
+    passed.wait()
+    for p in range(PARTS):
+        for copy in store(p):
+            copy.wait()
 
 
 def on_device(tokens, cotangent, combine, expert_ids, capacity, weight_in, weight_down):
     vmem = pl.BlockSpec(memory_space=pltpu.VMEM)
     hbm = pl.BlockSpec(memory_space=pl.ANY)
-    token_grad, combine_grad, inner, down = pl.pallas_call(
+    token_grad, combine_grad, own, arrived = pl.pallas_call(
         kernel,
         out_shape=(
             jax.ShapeDtypeStruct((TOK, D), BF16),
-            jax.ShapeDtypeStruct((TOK, 2), BF16),
-            jax.ShapeDtypeStruct((LOCAL, HALF, 2 * FF), F32),
-            jax.ShapeDtypeStruct((LOCAL, HALF, D), F32),
+            jax.ShapeDtypeStruct((2, TOK), BF16),
+            jax.ShapeDtypeStruct((LOCAL, HALF, WIDE), BF16),
+            jax.ShapeDtypeStruct((LOCAL, 2, HALF, WIDE), BF16),
         ),
-        in_specs=[vmem] * 5 + [hbm] * 2,
-        out_specs=(vmem,) * 4,
+        in_specs=[hbm] * 7,
+        out_specs=(vmem, vmem, hbm, hbm),
         scratch_shapes=[
+            pltpu.VMEM((TOK, D), BF16),
+            pltpu.VMEM((TOK, D), BF16),
+            pltpu.VMEM((2, TOK), F32),
+            pltpu.VMEM((2, TOK), jnp.int32),
+            pltpu.VMEM((1, EXPERTS), jnp.int32),
             pltpu.VMEM((2, STAGE, LOCAL, 2 * FF), BF16),
             pltpu.VMEM((2, STAGE, LOCAL, D), BF16),
             pltpu.VMEM((LOCAL, D, 2 * FF), BF16),
@@ -384,9 +448,9 @@
             pltpu.VMEM((4, 2, HALF, WIDE), BF16),
             pltpu.VMEM((LOCAL, 4, HALF, WIDE), BF16),
             pltpu.VMEM((LOCAL, 2, HALF // 2, WIDE), BF16),
-            pltpu.VMEM((LOCAL, 2, HALF, WIDE), BF16),
             pltpu.VMEM((LOCAL, PEERS, CAP, RET), BF16),
             pltpu.VMEM((LOCAL, PEERS, CAP, RET), BF16),
+            pltpu.SemaphoreType.DMA((5,)),
             pltpu.SemaphoreType.DMA((2, 2)),
             pltpu.SemaphoreType.DMA((LOCAL, PEERS)),
             pltpu.SemaphoreType.DMA((LOCAL, PEERS)),
@@ -396,18 +460,40 @@
             pltpu.SemaphoreType.DMA((LOCAL, 4)),
             pltpu.SemaphoreType.DMA((LOCAL, 6)),
             pltpu.SemaphoreType.DMA((LOCAL, 6)),
+            pltpu.SemaphoreType.DMA((LOCAL,)),
         ],
         compiler_params=pltpu.CompilerParams(
             collective_id=0, has_side_effects=True, vmem_limit_bytes=62 * 2**20
         ),
         name="moe_backward",
-    )(tokens, cotangent, combine, expert_ids, capacity.reshape(1, EXPERTS), weight_in, weight_down)
-    return (
-        token_grad,
-        combine_grad,
-        jnp.transpose(inner, (1, 0, 2)),
-        jnp.transpose(down, (1, 0, 2)),
+    )(
+        tokens, cotangent, combine.T, expert_ids.T, capacity.reshape(1, EXPERTS),
+        weight_in, weight_down,
     )
+    token_grad, combine_grad, inner, down = pl.pallas_call(
+        finish,
+        out_shape=(
+            jax.ShapeDtypeStruct((TOK, D), BF16),
+            jax.ShapeDtypeStruct((2, TOK), BF16),
+            jax.ShapeDtypeStruct((HALF, LOCAL, 2 * FF), F32),
+            jax.ShapeDtypeStruct((HALF, LOCAL, D), F32),
+        ),
+        in_specs=[hbm, vmem, hbm, hbm],
+        out_specs=(hbm, vmem, hbm, hbm),
+        scratch_shapes=[
+            pltpu.VMEM((TOK, D), BF16),
+            pltpu.VMEM((LOCAL, HALF, WIDE), BF16),
+            pltpu.VMEM((LOCAL, 2, HALF, WIDE), BF16),
+            pltpu.VMEM((HALF, LOCAL, 2 * FF), F32),
+            pltpu.VMEM((HALF, LOCAL, D), F32),
+            pltpu.SemaphoreType.DMA((2,)),
+            pltpu.SemaphoreType.DMA((2, PARTS)),
+            pltpu.SemaphoreType.DMA((2, PARTS)),
+        ],
+        compiler_params=pltpu.CompilerParams(vmem_limit_bytes=62 * 2**20),
+        name="finish_sums",
+    )(token_grad, combine_grad, own, arrived)
+    return token_grad, combine_grad.T, inner, down
 
 
 def solution(mesh):

time: 118 us -> 102 us (0.86)
  local copies, waits for them, and re-layouts: 12.8 us -> 0 us
  Pallas kernels: 104 us -> 101 us
    unnamed x8 -> x0, local copies, waits for them, and re-layouts: 12.8 us -> none
    pallas_call x1, Pallas kernels: 104 us -> 95.3 us  [on_device(): pl.pallas_call(kernel, out_shape=(jax.ShapeDtypeStruct((TOK, D), BF16), j...]
    pallas_call x0 -> x1, Pallas kernels: none -> 5.53 us  [on_device(): pl.pallas_call(finish, out_shape=(jax.ShapeDtypeStruct((TOK, D), BF16), j...]
where the time goes in v2:
time: 102 us
  Pallas kernels  101 us (99%)
    pallas_call x1, Pallas kernels, on_device(): pl.pallas_call(kernel, out_shape=(jax.ShapeDtypeStruct((TOK, D), BF16), j...  95.3 us
    pallas_call x1, Pallas kernels, on_device(): pl.pallas_call(finish, out_shape=(jax.ShapeDtypeStruct((TOK, D), BF16), j...  5.53 us

profile of v2, /device:TPU:1, one launch (start us, length us, event | category | flops | bytes accessed | tf_op | source)
XLA Modules:
  0.0 101.6 jit_solution(17795238096616971515)
XLA Ops:
  0.6 95.3 %moe_backward.1 = (bf16[256,1024]{1,0:T(8,128)(2,1)}, bf16[2,256]{1,0:T(2,128)(2,1)}, bf16[2,128,3072]{2,1,0:T(8,128)(2,1)}, bf16[2,2,128,3072]{3,2,1,0:T(8,128)(2,1)}) custom-call(bf16[256,1024]{1,0:T(8,128)(2,1)} %tokens_in.1, bf16[256,1024]{1,0:T(8,128)(2,1)} %cotangent_in.1, f32[2,256]{1,0:T(2,128)} %bitcast.4, s32[2,256]{1,0:T(2,128)} %bitcast.5, ...), custom_call_target="tpu_custom_call" | custom-call | tf_op jit(solution)/shard_map/moe_backward/pallas_call | solution.py:421
  95.9 5.5 %finish_sums.1 = (bf16[256,1024]{1,0:T(8,128)(2,1)}, bf16[2,256]{1,0:T(2,128)(2,1)}, f32[128,2,2048]{2,1,0:T(2,128)}, f32[128,2,1024]{2,1,0:T(2,128)}) custom-call(bf16[256,1024]{1,0:T(8,128)(2,1)} %get-tuple-element.12.token_in, bf16[2,256]{1,0:T(2,128)(2,1)} %get-tuple-element.13.combine_in, bf16[2,128,3072]{2,1,0:T(8,128)(2,1)} %get-tuple-element.14.own_in, ...), custom_call_target="tpu_custom_call" | custom-call | tf_op jit(solution)/shard_map/finish_sums/pallas_call | solution.py:473

commit v3 on v2

--- a/solution.py
+++ b/solution.py
@@ -21,6 +21,9 @@
 HALF = 128
 TILE = 256
 RET = D + 128
+GROUPS = 3
+GROUP = WIDE // GROUPS
+LAG = 3
 STAGE = 128
 PARTS = 4
 
@@ -80,26 +83,32 @@
             device_id=(dp, partner(i, -1)), device_id_type=MESH,
         )
 
-    def to_sibling(e, s):
+    def group_cols(q):
+        return pl.ds(q * GROUP, GROUP)
+
+    def to_sibling(e, s, q):
+        cols = group_cols(q)
         return pltpu.make_async_remote_copy(
-            src_ref=part.at[s, 1 - core], dst_ref=core_sum.at[e, s],
-            send_sem=core_send_sem.at[e, s], recv_sem=core_recv_sem.at[e, s],
+            src_ref=part.at[s, 1 - core, :, cols], dst_ref=core_sum.at[e, s, :, cols],
+            send_sem=core_send_sem.at[e, s, q], recv_sem=core_recv_sem.at[e, s, q],
             device_id=sibling, device_id_type=MESH,
         )
 
     half = HALF // 2
 
-    def z_copy(e, k):
+    def z_copy(e, k, q):
+        cols, low, high = group_cols(q), pl.ds(0, half), pl.ds(half, half)
         src, dst, step = (
-            (core_sum.at[e, 0, pl.ds(0, half)], relay.at[e, 0], 1),
-            (core_sum.at[e, 0, pl.ds(half, half)], relay.at[e, 1], 3),
-            (core_sum.at[e, 1, pl.ds(half, half)], arrived.at[e, 0, pl.ds(half, half)], 1),
-            (core_sum.at[e, 2, pl.ds(0, half)], arrived.at[e, 1, pl.ds(0, half)], 3),
-            (core_sum.at[e, 1, pl.ds(0, half)], arrived.at[e, 0, pl.ds(0, half)], 1),
-            (core_sum.at[e, 2, pl.ds(half, half)], arrived.at[e, 1, pl.ds(half, half)], 3),
+            (core_sum.at[e, 0, low, cols], relay.at[e, 0, :, cols], 1),
+            (core_sum.at[e, 0, high, cols], relay.at[e, 1, :, cols], 3),
+            (core_sum.at[e, 1, high, cols], arrived.at[e, 0, high, cols], 1),
+            (core_sum.at[e, 2, low, cols], arrived.at[e, 1, low, cols], 3),
+            (core_sum.at[e, 1, low, cols], arrived.at[e, 0, low, cols], 1),
+            (core_sum.at[e, 2, high, cols], arrived.at[e, 1, high, cols], 3),
         )[k]
         return pltpu.make_async_remote_copy(
-            src_ref=src, dst_ref=dst, send_sem=z_send_sem.at[e, k], recv_sem=z_recv_sem.at[e, k],
+            src_ref=src, dst_ref=dst,
+            send_sem=z_send_sem.at[e, k, q], recv_sem=z_recv_sem.at[e, k, q],
             device_id=along_z(step), device_id_type=MESH,
         )
 
@@ -157,10 +166,13 @@
     for i in range(PEERS):
         first = jnp.where(slot_lane // CAP == i, partner(i, 1) * (LOCAL * CAP), first)
     first = first + slot_lane % CAP
-    for e in range(LOCAL):
+
+    def choose(e):
         wanted = first + e * CAP
         pick0[e] = (target0 == wanted).astype(F32).astype(BF16)
         pick1[e] = (target1 == wanted).astype(F32).astype(BF16)
+
+    choose(0)
 
     def gather(e, group):
         lanes = pl.ds(group * 128, 128)
@@ -189,6 +201,7 @@
         if group == 0:
             pl.semaphore_wait(barrier, len(greeted))
         start_dispatch(0, group * 4, group * 4 + 4)
+    choose(1)
     for group in range(4):
         gather(1, group)
 
@@ -247,59 +260,62 @@
             buffer = ret_recv if i == 0 else ret_send
             buffer[e, i, :, D:RET] = total[j]
 
-    def partial(e, s):
+    def partial(e, s, q):
         at = pl.multiple_of(((z + STEPS[s]) % 4) * TILE, TILE)
-        turned[...] = recv[e, :, 0:CAP, pl.ds(at, TILE)].reshape(SLOTS, TILE).T
-
-        def inner_tile(n, _):
-            cols = pl.ds(pl.multiple_of(n * TILE, TILE), TILE)
-            part[s, :, :, cols] = dot(turned[...], dpre[:, cols]).astype(BF16).reshape(2, HALF, TILE)
-            return 0
-
-        lax.fori_loop(0, 2 * FF // TILE, inner_tile, 0, unroll=True)
-        turned[...] = hidden[:, pl.ds(at, TILE)].T
-
-        def down_tile(n, _):
+        if q == 0:
+            turned[...] = recv[e, :, 0:CAP, pl.ds(at, TILE)].reshape(SLOTS, TILE).T
+        if q == 2:
+            turned[...] = hidden[:, pl.ds(at, TILE)].T
+
+        def tile(n, _):
             at = pl.multiple_of(n * TILE, TILE)
-            scaled = recv[e, :, CAP:2 * CAP, pl.ds(at, TILE)].reshape(SLOTS, TILE)
-            part[s, :, :, pl.ds(2 * FF + at, TILE)] = (
-                dot(turned[...], scaled).astype(BF16).reshape(2, HALF, TILE)
+            if q < 2:
+                other = dpre[:, pl.ds(q * GROUP + at, TILE)]
+            else:
+                other = recv[e, :, CAP:2 * CAP, pl.ds(at, TILE)].reshape(SLOTS, TILE)
+            part[s, :, :, pl.ds(q * GROUP + at, TILE)] = (
+                dot(turned[...], other).astype(BF16).reshape(2, HALF, TILE)
             )
             return 0
 
-        lax.fori_loop(0, D // TILE, down_tile, 0, unroll=True)
-
-    def add_rows(dst, lo, count, other):
+        lax.fori_loop(0, GROUP // TILE, tile, 0, unroll=True)
+
+    def add_rows(dst, lo, count, other, q):
+        cols = group_cols(q)
+
         def block(b, _):
             at = pl.multiple_of(b * 16, 16)
-            here = dst[pl.ds(lo + at, 16)].astype(F32)
-            dst[pl.ds(lo + at, 16)] = (here + other[pl.ds(at, 16)].astype(F32)).astype(BF16)
+            here = dst[pl.ds(lo + at, 16), cols].astype(F32)
+            there = other[pl.ds(at, 16), cols].astype(F32)
+            dst[pl.ds(lo + at, 16), cols] = (here + there).astype(BF16)
             return 0
 
         lax.fori_loop(0, count // 16, block, 0)
 
-    def meet_sibling(e, s):
-        to_sibling(e, s).wait_recv()
-        add_rows(core_sum.at[e, s], 0, HALF, part.at[s, core])
+    def meet_sibling(e, s, q):
+        to_sibling(e, s, q).wait_recv()
+        add_rows(core_sum.at[e, s], 0, HALF, part.at[s, core], q)
         for k in ((0, 1), (2,), (3,), ())[s]:
-            z_copy(e, k).start()
+            z_copy(e, k, q).start()
 
     def weight_sums(e):
-        for s in range(4):
-            partial(e, s)
-            to_sibling(e, s).start()
-            if s > 0:
-                meet_sibling(e, s - 1)
-        meet_sibling(e, 3)
+        units = [(s, q) for s in range(4) for q in range(GROUPS)]
+        for n, unit in enumerate(units):
+            partial(e, *unit)
+            to_sibling(e, *unit).start()
+            if n >= LAG:
+                meet_sibling(e, *units[n - LAG])
+        for unit in units[-LAG:]:
+            meet_sibling(e, *unit)
         keep(e).start()
 
-    def pass_on(e):
-        z_copy(e, 0).wait_recv()
-        add_rows(core_sum.at[e, 1], 0, half, relay.at[e, 0])
-        z_copy(e, 4).start()
-        z_copy(e, 1).wait_recv()
-        add_rows(core_sum.at[e, 2], half, half, relay.at[e, 1])
-        z_copy(e, 5).start()
+    def pass_on(e, q):
+        z_copy(e, 0, q).wait_recv()
+        add_rows(core_sum.at[e, 1], 0, half, relay.at[e, 0], q)
+        z_copy(e, 4, q).start()
+        z_copy(e, 1, q).wait_recv()
+        add_rows(core_sum.at[e, 2], half, half, relay.at[e, 1], q)
+        z_copy(e, 5, q).start()
 
     def input_grad(e, h):
         def tile(n, _):
@@ -316,20 +332,30 @@
         for i in range(max(h * 8, 1), h * 8 + 8):
             give_back(e, i).start()
 
-    for e in range(LOCAL):
-        arrive(e, 0, 8)
-        if e == 0:
-            start_dispatch(1, 0, PEERS)
-        forward(e, 0)
-        arrive(e, 8, PEERS)
-        forward(e, 1)
-        if e == 1:
-            for s in range(4):
-                to_sibling(0, s).wait_send()
-        weight_sums(e)
-        input_grad(e, 0)
-        pass_on(e)
-        input_grad(e, 1)
+    arrive(0, 0, 8)
+    start_dispatch(1, 0, PEERS)
+    forward(0, 0)
+    arrive(0, 8, PEERS)
+    forward(0, 1)
+    weight_sums(0)
+    input_grad(0, 0)
+    input_grad(0, 1)
+    pass_on(0, 0)
+    arrive(1, 0, 8)
+    forward(1, 0)
+    pass_on(0, 1)
+    pass_on(0, 2)
+    arrive(1, 8, PEERS)
+    forward(1, 1)
+    for s in range(4):
+        for q in range(GROUPS):
+            to_sibling(0, s, q).wait_send()
+    weight_sums(1)
+    input_grad(1, 0)
+    pass_on(1, 0)
+    input_grad(1, 1)
+    pass_on(1, 1)
+    pass_on(1, 2)
 
     for e in range(LOCAL):
         for i in range(1, PEERS):
@@ -355,13 +381,15 @@
         for i in range(1, PEERS):
             dispatch(e, i).wait_send()
             give_back(e, i).wait_send()
-        for k in range(6):
-            z_copy(e, k).wait_send()
-        for k in (2, 3, 4, 5):
-            z_copy(e, k).wait_recv()
+        for q in range(GROUPS):
+            for k in range(6):
+                z_copy(e, k, q).wait_send()
+            for k in (2, 3, 4, 5):
+                z_copy(e, k, q).wait_recv()
         keep(e).wait()
     for s in range(4):
-        to_sibling(1, s).wait_send()
+        for q in range(GROUPS):
+            to_sibling(1, s, q).wait_send()
 
 
 def finish(
@@ -456,10 +484,10 @@
             pltpu.SemaphoreType.DMA((LOCAL, PEERS)),
             pltpu.SemaphoreType.DMA((LOCAL, PEERS)),
             pltpu.SemaphoreType.DMA((LOCAL, PEERS)),
-            pltpu.SemaphoreType.DMA((LOCAL, 4)),
-            pltpu.SemaphoreType.DMA((LOCAL, 4)),
-            pltpu.SemaphoreType.DMA((LOCAL, 6)),
-            pltpu.SemaphoreType.DMA((LOCAL, 6)),
+            pltpu.SemaphoreType.DMA((LOCAL, 4, GROUPS)),
+            pltpu.SemaphoreType.DMA((LOCAL, 4, GROUPS)),
+            pltpu.SemaphoreType.DMA((LOCAL, 6, GROUPS)),
+            pltpu.SemaphoreType.DMA((LOCAL, 6, GROUPS)),
             pltpu.SemaphoreType.DMA((LOCAL,)),
         ],
         compiler_params=pltpu.CompilerParams(

time: 102 us -> 101 us (level)
  no operation moved by 1% of the time
where the time goes in v3:
time: 101 us
  Pallas kernels  100 us (99%)
    pallas_call x1, Pallas kernels, on_device(): pl.pallas_call(kernel, out_shape=(jax.ShapeDtypeStruct((TOK, D), BF16), j...  94.8 us
    pallas_call x1, Pallas kernels, on_device(): pl.pallas_call(finish, out_shape=(jax.ShapeDtypeStruct((TOK, D), BF16), j...  5.53 us

profile of v3, /device:TPU:1, one launch (start us, length us, event | category | flops | bytes accessed | tf_op | source)
XLA Modules:
  0.0 101.1 jit_solution(2091383225013923430)
XLA Ops:
  0.6 94.8 %moe_backward.1 = (bf16[256,1024]{1,0:T(8,128)(2,1)}, bf16[2,256]{1,0:T(2,128)(2,1)}, bf16[2,128,3072]{2,1,0:T(8,128)(2,1)}, bf16[2,2,128,3072]{3,2,1,0:T(8,128)(2,1)}) custom-call(bf16[256,1024]{1,0:T(8,128)(2,1)} %tokens_in.1, bf16[256,1024]{1,0:T(8,128)(2,1)} %cotangent_in.1, f32[2,256]{1,0:T(2,128)} %bitcast.4, s32[2,256]{1,0:T(2,128)} %bitcast.5, ...), custom_call_target="tpu_custom_call" | custom-call | tf_op jit(solution)/shard_map/moe_backward/pallas_call | solution.py:449
  95.4 5.5 %finish_sums.1 = (bf16[256,1024]{1,0:T(8,128)(2,1)}, bf16[2,256]{1,0:T(2,128)(2,1)}, f32[128,2,2048]{2,1,0:T(2,128)}, f32[128,2,1024]{2,1,0:T(2,128)}) custom-call(bf16[256,1024]{1,0:T(8,128)(2,1)} %get-tuple-element.12.token_in, bf16[2,256]{1,0:T(2,128)(2,1)} %get-tuple-element.13.combine_in, bf16[2,128,3072]{2,1,0:T(8,128)(2,1)} %get-tuple-element.14.own_in, ...), custom_call_target="tpu_custom_call" | custom-call | tf_op jit(solution)/shard_map/finish_sums/pallas_call | solution.py:501
